TPU v7x, 32 devices: a whole 2x2x4 slice. The times are simulated.
32 devices in a mesh: gx: 2 (over core), gy: 4 (over y, x), gz: 4 (over z).
Axes of the slice: x: 2, y: 2, z: 4, core: 2. Of those that a mesh axis runs over, the one named last changes fastest.
Arguments:
- basis: bfloat16 [2, 4, 4, 96, 6144], P('gx', 'gy', 'gz'), may hold values from -0.078125 to 0.078125
- diagonal: float32 [2, 4, 4, 6144], P('gx', 'gy', 'gz'), may hold values from 0.05 to 1
- source: float32 [2, 4, 4, 16, 96], P('gx', 'gy', 'gz'), may hold values from -6 to 6
- well_cells: int32 [2, 4, 4, 16], P('gx', 'gy', 'gz'), may hold values from 0 to 95
Outputs:
- solution_field: float32 [2, 4, 4, 16, 3072], P('gx', 'gy', 'gz')
All inputs are finite; a program needn't handle non-finite values.
Results may differ from a plain program's by a relative error of at most 0.0036.
Values sent between devices are 32-bit elements; how exact they have to be, the bound alone decides.
A program may use at most 64 MiB of HBM per device.

v0:
```python
import jax
import jax.numpy as jnp
from jax import lax
from jax.sharding import PartitionSpec as P

ITERS = 2


well_rate = 4.0


def passed_along(value, axis, steps):
    count = lax.axis_size(axis)
    leading, last = (max(0, -steps), min(count, count - steps))
    return lax.ppermute(value, axis, [(source, source + steps) for source in range(leading, last)])


def respond(vector, basis_local, diag_local):
    mode_values = lax.dot_general(
        vector.astype(jnp.bfloat16),
        basis_local,
        (((1,), (1,)), ((), ())),
        preferred_element_type=jnp.float32,
    ).astype(jnp.bfloat16)
    return diag_local * vector + jnp.dot(
        mode_values, basis_local, preferred_element_type=jnp.float32
    )


def widen_field(owned_field, face_width, layout):
    uppers = []
    for which_axis, stride, position, extent in layout:
        lower_face = owned_field[:, which_axis * face_width : (which_axis + 1) * face_width]
        arrived = passed_along(lower_face, ("gx", "gy", "gz"), -stride)
        uppers.append(jnp.where(position < extent - 1, arrived, 0.0))
    return jnp.concatenate([owned_field] + uppers, axis=1)


def lower_jumps(responses, face_width, layout):
    face_parts = []
    for which_axis, stride, position, extent in layout:
        lower_face = responses[:, which_axis * face_width : (which_axis + 1) * face_width]
        upper_face = responses[:, (3 + which_axis) * face_width : (4 + which_axis) * face_width]
        from_below = passed_along(upper_face, ("gx", "gy", "gz"), stride)
        face_parts.append(jnp.where(position > 0, lower_face + from_below, 0.0))
    return jnp.concatenate(face_parts, axis=1)


def body(basis, diagonal, source, well_cells):
    basis_local = basis[0, 0, 0]
    diag_local = diagonal[0, 0, 0]
    source_local = source[0, 0, 0]
    wells_local = well_cells[0, 0, 0]
    face_width = basis_local.shape[1] // 6
    layout = (
        (0, lax.axis_size("gy") * lax.axis_size("gz"), lax.axis_index("gx"), lax.axis_size("gx")),
        (1, lax.axis_size("gz"), lax.axis_index("gy"), lax.axis_size("gy")),
        (2, 1, lax.axis_index("gz"), lax.axis_size("gz")),
    )
    well_picks = lax.broadcasted_iota(jnp.int32, source_local.shape, 1) == wells_local[:, None]
    load_low = (source_local + well_rate * well_picks.astype(jnp.float32)).astype(jnp.bfloat16)
    load_flux = jnp.dot(load_low, basis_local, preferred_element_type=jnp.float32)

    def operate(vector):
        return lower_jumps(
            respond(widen_field(vector, face_width, layout), basis_local, diag_local),
            face_width,
            layout,
        )

    right_side = lower_jumps(load_flux, face_width, layout)

    def local_inner(left_field, right_field):
        return jnp.sum(left_field * right_field, axis=1)

    solution_field = jnp.zeros_like(right_side)

    def squares(vector):
        return lax.psum(local_inner(vector, vector), ("gx", "gy", "gz"))

    def advance(iteration, loop_state):
        solution_field, residual, direction, norm_now = loop_state
        applied = operate(direction)
        curvature = lax.psum(local_inner(direction, applied), ("gx", "gy", "gz"))
        step_size = (norm_now / curvature)[:, None]
        solution_field = solution_field + step_size * direction
        residual = residual - step_size * applied
        norm_next = squares(residual)
        direction = residual + (norm_next / norm_now)[:, None] * direction
        return (solution_field, residual, direction, norm_next)

    loop_state = lax.fori_loop(
        0, ITERS, advance, (solution_field, right_side, right_side, squares(right_side))
    )
    solution_field = loop_state[0]
    return solution_field[None, None, None]


def solution(mesh):
    in_specs = (
        P("gx", "gy", "gz", None, None),
        P("gx", "gy", "gz", None),
        P("gx", "gy", "gz", None, None),
        P("gx", "gy", "gz", None),
    )
    out_specs = P("gx", "gy", "gz", None, None)
    return jax.shard_map(body, mesh=mesh, in_specs=in_specs, out_specs=out_specs, check_vma=False)
```

profile of v0, /device:TPU:0, one launch (start us, length us, event | category | flops | bytes accessed | tf_op | source)
XLA Modules:
  0.0 272.5 jit_solution(8366613316968730645)
XLA Ops:
  0.0 1.6 fusion.15
  1.7 2.5 collective-permute-start.6
  4.2 0.9 collective-permute-done.6
  5.1 4.2 %collective-permute-start.7 = (f32[16,1024]{1,0:T(8,128)S(1)}, f32[16,1024]{1,0:T(8,128)S(1)}, u32[]{:S(2)}, u32[]{:S(2)}) collective-permute-start(f32[16,1024]{1,0:T(8,128)S(1)} %get-tuple-element.223), channel_id=1, source_target_pairs={{0,4},{1,5},{2,6},{3,7},{4,8},{5,9},{6,10},{7,11},{8,12},{9,13},{1... | collective-permute-start | bytes 196616 | tf_op jit(solution)/shard_map/ppermute | solution.py:15
  9.3 3.5 %collective-permute-start.8 = (f32[16,1024]{1,0:T(8,128)S(1)}, f32[16,1024]{1,0:T(8,128)S(1)}, u32[]{:S(2)}, u32[]{:S(2)}) collective-permute-start(f32[16,1024]{1,0:T(8,128)S(1)} %get-tuple-element.222), channel_id=1, source_target_pairs={{0,1},{1,2},{2,3},{3,4},{4,5},{5,6},{6,7},{7,8},{8,9},{9,10},{10,1... | collective-permute-start | bytes 196616 | tf_op jit(solution)/shard_map/ppermute | solution.py:15
  12.8 0.0 collective-permute-done.7
  12.8 1.8 collective-permute-done.8
  14.7 0.1 multiply_reduce_fusion.2
  14.8 40.8 %psum.25 = f32[16]{0:T(128)S(1)} all-reduce(f32[16]{0:T(128)S(1)} %get-tuple-element.226), channel_id=1, replica_groups=mesh['gx'=2,'gy'=4,'gz'=4] {'gx','gy','gz'}, use_global_device_ids=true, to_apply=%region_1.2 | all-reduce | flops 16 | bytes 128 | tf_op jit(solution)/shard_map/psum | solution.py:79
  55.6 216.2 %while.19 = (s32[]{:T(128)}, f32[16,3072]{1,0:T(8,128)S(1)}, f32[16,3072]{1,0:T(8,128)S(1)}, f32[16,3072]{1,0:T(8,128)S(1)}, f32[16]{0:T(128)S(1)}, /*index=5*/p...) while((s32[]{:T(128)}, f32[16,3072]{1,0:T(8,128)S(1)}, ...), condition=%wide.region_7.8_spmd.clone, body=%wide.region_2.7_spmd.clone.sunk | while | flops 39519776 | bytes 7300557 | solution.py:92
  55.7 1.3 collective-permute-start
  57.0 1.3 collective-permute-start.1
  58.3 1.3 collective-permute-start.2
  59.6 3.1 %collective-permute-done = f32[16,1024]{1,0:T(8,128)S(1)} collective-permute-done((f32[16,1024]{1,0:T(8,128)S(1)}, f32[16,1024]{1,0:T(8,128)S(1)}, u32[]{:S(2)}, u32[]{:S(2)}) %collective-permute-start) | collective-permute-done | bytes 65568 | tf_op jit(solution)/shard_map/while/body/eval_jaxpr/ppermute | solution.py:15
  62.7 2.8 %collective-permute-done.1 = f32[16,1024]{1,0:T(8,128)S(1)} collective-permute-done((f32[16,1024]{1,0:T(8,128)S(1)}, f32[16,1024]{1,0:T(8,128)S(1)}, u32[]{:S(2)}, u32[]{:S(2)}) %collective-permute-start.1) | collective-permute-done | bytes 65568 | tf_op jit(solution)/shard_map/while/body/eval_jaxpr/ppermute | solution.py:15
  65.5 1.6 collective-permute-done.2
  67.1 1.0 multiply_add_fusion.4
  68.1 3.0 %collective-permute-start.3 = (f32[16,1024]{1,0:T(8,128)S(1)}, f32[16,1024]{1,0:T(8,128)S(1)}, u32[]{:S(2)}, u32[]{:S(2)}) collective-permute-start(f32[16,1024]{1,0:T(8,128)S(1)} %slice.130), channel_id=1, source_target_pairs={{0,16},{1,17},{2,18},{3,19},{4,20},{5,21},{6,22},{7,23},{8,24},{9,... | collective-permute-start | bytes 196616 | tf_op jit(solution)/shard_map/while/body/eval_jaxpr/ppermute | solution.py:15
  71.1 0.9 collective-permute-done.3
  72.0 2.7 collective-permute-start.4
  74.7 2.1 collective-permute-start.5
  76.9 0.0 collective-permute-done.4
  76.9 1.9 collective-permute-done.5
  78.8 0.1 multiply_reduce_fusion.5
  78.9 42.4 %psum.30 = f32[16]{0:T(128)S(1)} all-reduce(f32[16]{0:T(128)S(1)} %multiply_reduce_fusion.5), channel_id=1, replica_groups=mesh['gx'=2,'gy'=4,'gz'=4] {'gx','gy','gz'}, use_global_device_ids=true, to_apply=%region_4.4 | all-reduce | flops 16 | bytes 128 | tf_op jit(solution)/shard_map/while/body/eval_jaxpr/psum | solution.py:84
  121.3 0.3 multiply_reduce_fusion.6
  121.6 42.4 %psum.31 = f32[16]{0:T(128)S(1)} all-reduce(f32[16]{0:T(128)S(1)} %get-tuple-element.328), channel_id=1, replica_groups=mesh['gx'=2,'gy'=4,'gz'=4] {'gx','gy','gz'}, use_global_device_ids=true, to_apply=%region_6.6 | all-reduce | flops 16 | bytes 128 | tf_op jit(solution)/shard_map/while/body/eval_jaxpr/psum | solution.py:79
  163.9 0.1 multiply_add_fusion.5
  164.1 1.3 collective-permute-start
  165.4 1.3 collective-permute-start.1
  166.7 1.3 collective-permute-start.2
  168.0 2.3 collective-permute-done
  170.3 2.9 %collective-permute-done.1 = f32[16,1024]{1,0:T(8,128)S(1)} collective-permute-done((f32[16,1024]{1,0:T(8,128)S(1)}, f32[16,1024]{1,0:T(8,128)S(1)}, u32[]{:S(2)}, u32[]{:S(2)}) %collective-permute-start.1) | collective-permute-done | bytes 65568 | tf_op jit(solution)/shard_map/while/body/eval_jaxpr/ppermute | solution.py:15
  173.2 1.6 collective-permute-done.2
  174.8 1.0 multiply_add_fusion.4
  175.8 2.1 collective-permute-start.3
  177.9 0.9 collective-permute-done.3
  178.8 2.7 %collective-permute-start.4 = (f32[16,1024]{1,0:T(8,128)S(1)}, f32[16,1024]{1,0:T(8,128)S(1)}, u32[]{:S(2)}, u32[]{:S(2)}) collective-permute-start(f32[16,1024]{1,0:T(8,128)S(1)} %get-tuple-element.322), channel_id=1, source_target_pairs={{0,4},{1,5},{2,6},{3,7},{4,8},{5,9},{6,10},{7,11},{8,12},{9,13},{1... | collective-permute-start | bytes 196616 | tf_op jit(solution)/shard_map/while/body/eval_jaxpr/ppermute | solution.py:15
  181.5 2.9 %collective-permute-start.5 = (f32[16,1024]{1,0:T(8,128)S(1)}, f32[16,1024]{1,0:T(8,128)S(1)}, u32[]{:S(2)}, u32[]{:S(2)}) collective-permute-start(f32[16,1024]{1,0:T(8,128)S(1)} %get-tuple-element.323), channel_id=1, source_target_pairs={{0,1},{1,2},{2,3},{3,4},{4,5},{5,6},{6,7},{7,8},{8,9},{9,10},{10,1... | collective-permute-start | bytes 196616 | tf_op jit(solution)/shard_map/while/body/eval_jaxpr/ppermute | solution.py:15
  184.5 0.0 collective-permute-done.4
  184.5 1.9 collective-permute-done.5
  186.4 0.1 multiply_reduce_fusion.5
  186.5 42.0 %psum.30 = f32[16]{0:T(128)S(1)} all-reduce(f32[16]{0:T(128)S(1)} %multiply_reduce_fusion.5), channel_id=1, replica_groups=mesh['gx'=2,'gy'=4,'gz'=4] {'gx','gy','gz'}, use_global_device_ids=true, to_apply=%region_4.4 | all-reduce | flops 16 | bytes 128 | tf_op jit(solution)/shard_map/while/body/eval_jaxpr/psum | solution.py:84
  228.6 0.3 multiply_reduce_fusion.6
  228.8 42.9 %psum.31 = f32[16]{0:T(128)S(1)} all-reduce(f32[16]{0:T(128)S(1)} %get-tuple-element.328), channel_id=1, replica_groups=mesh['gx'=2,'gy'=4,'gz'=4] {'gx','gy','gz'}, use_global_device_ids=true, to_apply=%region_6.6 | all-reduce | flops 16 | bytes 128 | tf_op jit(solution)/shard_map/while/body/eval_jaxpr/psum | solution.py:79
  271.7 0.1 multiply_add_fusion.5
  271.9 0.0 copy-start.1
  271.9 0.7 copy-done.1
  (29 shorter events, 0.2 us)
Async XLA Ops:
  1.6 54.0 %copy-start = (bf16[1,1,1,96,6144]{4,3,2,1,0:T(8,128)(2,1)S(1)}, bf16[1,1,1,96,6144]{4,3,2,1,0:T(8,128)(2,1)}, u32[]{:S(2)}) copy-start(bf16[1,1,1,96,6144]{4,3,2,1,0:T(8,128)(2,1)} %param.6) | copy-start | bytes 3538948
  1.6 54.0 %copy-start.2 = (f32[1,1,1,6144]{3,2,1,0:T(1,128)S(1)}, f32[1,1,1,6144]{3,2,1,0:T(1,128)}, u32[]{:S(2)}) copy-start(f32[1,1,1,6144]{3,2,1,0:T(1,128)} %param.7) | copy-start | bytes 73732
  1.7 3.4 %collective-permute-start.6 = (f32[16,1024]{1,0:T(8,128)S(1)}, f32[16,1024]{1,0:T(8,128)S(1)}, u32[]{:S(2)}, u32[]{:S(2)}) collective-permute-start(f32[16,1024]{1,0:T(8,128)S(1)} %slice.85), channel_id=1, source_target_pairs={{0,16},{1,17},{2,18},{3,19},{4,20},{5,21},{6,22},{7,23},{8,24},{9,... | collective-permute-start | bytes 196616 | tf_op jit(solution)/shard_map/ppermute | solution.py:15
  5.1 7.8 %collective-permute-start.7 = (f32[16,1024]{1,0:T(8,128)S(1)}, f32[16,1024]{1,0:T(8,128)S(1)}, u32[]{:S(2)}, u32[]{:S(2)}) collective-permute-start(f32[16,1024]{1,0:T(8,128)S(1)} %get-tuple-element.223), channel_id=1, source_target_pairs={{0,4},{1,5},{2,6},{3,7},{4,8},{5,9},{6,10},{7,11},{8,12},{9,13},{1... | collective-permute-start | bytes 196616 | tf_op jit(solution)/shard_map/ppermute | solution.py:15
  9.3 5.4 %collective-permute-start.8 = (f32[16,1024]{1,0:T(8,128)S(1)}, f32[16,1024]{1,0:T(8,128)S(1)}, u32[]{:S(2)}, u32[]{:S(2)}) collective-permute-start(f32[16,1024]{1,0:T(8,128)S(1)} %get-tuple-element.222), channel_id=1, source_target_pairs={{0,1},{1,2},{2,3},{3,4},{4,5},{5,6},{6,7},{7,8},{8,9},{9,10},{10,1... | collective-permute-start | bytes 196616 | tf_op jit(solution)/shard_map/ppermute | solution.py:15
  55.7 7.0 %collective-permute-start = (f32[16,1024]{1,0:T(8,128)S(1)}, f32[16,1024]{1,0:T(8,128)S(1)}, u32[]{:S(2)}, u32[]{:S(2)}) collective-permute-start(f32[16,1024]{1,0:T(8,128)S(1)} %get-tuple-element.319), channel_id=1, source_target_pairs={{1,0},{2,1},{3,2},{4,3},{5,4},{6,5},{7,6},{8,7},{9,8},{10,9},{11,1... | collective-permute-start | bytes 196616 | tf_op jit(solution)/shard_map/while/body/eval_jaxpr/ppermute | solution.py:15
  57.0 8.5 %collective-permute-start.1 = (f32[16,1024]{1,0:T(8,128)S(1)}, f32[16,1024]{1,0:T(8,128)S(1)}, u32[]{:S(2)}, u32[]{:S(2)}) collective-permute-start(f32[16,1024]{1,0:T(8,128)S(1)} %get-tuple-element.320), channel_id=1, source_target_pairs={{4,0},{5,1},{6,2},{7,3},{8,4},{9,5},{10,6},{11,7},{12,8},{13,9},{1... | collective-permute-start | bytes 196616 | tf_op jit(solution)/shard_map/while/body/eval_jaxpr/ppermute | solution.py:15
  58.3 8.8 %collective-permute-start.2 = (f32[16,1024]{1,0:T(8,128)S(1)}, f32[16,1024]{1,0:T(8,128)S(1)}, u32[]{:S(2)}, u32[]{:S(2)}) collective-permute-start(f32[16,1024]{1,0:T(8,128)S(1)} %get-tuple-element.321), channel_id=1, source_target_pairs={{16,0},{17,1},{18,2},{19,3},{20,4},{21,5},{22,6},{23,7},{24,8},{25... | collective-permute-start | bytes 196616 | tf_op jit(solution)/shard_map/while/body/eval_jaxpr/ppermute | solution.py:15
  68.1 3.9 %collective-permute-start.3 = (f32[16,1024]{1,0:T(8,128)S(1)}, f32[16,1024]{1,0:T(8,128)S(1)}, u32[]{:S(2)}, u32[]{:S(2)}) collective-permute-start(f32[16,1024]{1,0:T(8,128)S(1)} %slice.130), channel_id=1, source_target_pairs={{0,16},{1,17},{2,18},{3,19},{4,20},{5,21},{6,22},{7,23},{8,24},{9,... | collective-permute-start | bytes 196616 | tf_op jit(solution)/shard_map/while/body/eval_jaxpr/ppermute | solution.py:15
  72.0 4.9 %collective-permute-start.4 = (f32[16,1024]{1,0:T(8,128)S(1)}, f32[16,1024]{1,0:T(8,128)S(1)}, u32[]{:S(2)}, u32[]{:S(2)}) collective-permute-start(f32[16,1024]{1,0:T(8,128)S(1)} %get-tuple-element.322), channel_id=1, source_target_pairs={{0,4},{1,5},{2,6},{3,7},{4,8},{5,9},{6,10},{7,11},{8,12},{9,13},{1... | collective-permute-start | bytes 196616 | tf_op jit(solution)/shard_map/while/body/eval_jaxpr/ppermute | solution.py:15
  74.7 4.0 %collective-permute-start.5 = (f32[16,1024]{1,0:T(8,128)S(1)}, f32[16,1024]{1,0:T(8,128)S(1)}, u32[]{:S(2)}, u32[]{:S(2)}) collective-permute-start(f32[16,1024]{1,0:T(8,128)S(1)} %get-tuple-element.323), channel_id=1, source_target_pairs={{0,1},{1,2},{2,3},{3,4},{4,5},{5,6},{6,7},{7,8},{8,9},{9,10},{10,1... | collective-permute-start | bytes 196616 | tf_op jit(solution)/shard_map/while/body/eval_jaxpr/ppermute | solution.py:15
  164.1 6.2 %collective-permute-start = (f32[16,1024]{1,0:T(8,128)S(1)}, f32[16,1024]{1,0:T(8,128)S(1)}, u32[]{:S(2)}, u32[]{:S(2)}) collective-permute-start(f32[16,1024]{1,0:T(8,128)S(1)} %get-tuple-element.319), channel_id=1, source_target_pairs={{1,0},{2,1},{3,2},{4,3},{5,4},{6,5},{7,6},{8,7},{9,8},{10,9},{11,1... | collective-permute-start | bytes 196616 | tf_op jit(solution)/shard_map/while/body/eval_jaxpr/ppermute | solution.py:15
  165.4 7.8 %collective-permute-start.1 = (f32[16,1024]{1,0:T(8,128)S(1)}, f32[16,1024]{1,0:T(8,128)S(1)}, u32[]{:S(2)}, u32[]{:S(2)}) collective-permute-start(f32[16,1024]{1,0:T(8,128)S(1)} %get-tuple-element.320), channel_id=1, source_target_pairs={{4,0},{5,1},{6,2},{7,3},{8,4},{9,5},{10,6},{11,7},{12,8},{13,9},{1... | collective-permute-start | bytes 196616 | tf_op jit(solution)/shard_map/while/body/eval_jaxpr/ppermute | solution.py:15
  166.7 8.1 %collective-permute-start.2 = (f32[16,1024]{1,0:T(8,128)S(1)}, f32[16,1024]{1,0:T(8,128)S(1)}, u32[]{:S(2)}, u32[]{:S(2)}) collective-permute-start(f32[16,1024]{1,0:T(8,128)S(1)} %get-tuple-element.321), channel_id=1, source_target_pairs={{16,0},{17,1},{18,2},{19,3},{20,4},{21,5},{22,6},{23,7},{24,8},{25... | collective-permute-start | bytes 196616 | tf_op jit(solution)/shard_map/while/body/eval_jaxpr/ppermute | solution.py:15
  175.8 2.9 %collective-permute-start.3 = (f32[16,1024]{1,0:T(8,128)S(1)}, f32[16,1024]{1,0:T(8,128)S(1)}, u32[]{:S(2)}, u32[]{:S(2)}) collective-permute-start(f32[16,1024]{1,0:T(8,128)S(1)} %slice.130), channel_id=1, source_target_pairs={{0,16},{1,17},{2,18},{3,19},{4,20},{5,21},{6,22},{7,23},{8,24},{9,... | collective-permute-start | bytes 196616 | tf_op jit(solution)/shard_map/while/body/eval_jaxpr/ppermute | solution.py:15
  178.8 5.7 %collective-permute-start.4 = (f32[16,1024]{1,0:T(8,128)S(1)}, f32[16,1024]{1,0:T(8,128)S(1)}, u32[]{:S(2)}, u32[]{:S(2)}) collective-permute-start(f32[16,1024]{1,0:T(8,128)S(1)} %get-tuple-element.322), channel_id=1, source_target_pairs={{0,4},{1,5},{2,6},{3,7},{4,8},{5,9},{6,10},{7,11},{8,12},{9,13},{1... | collective-permute-start | bytes 196616 | tf_op jit(solution)/shard_map/while/body/eval_jaxpr/ppermute | solution.py:15
  181.5 4.8 %collective-permute-start.5 = (f32[16,1024]{1,0:T(8,128)S(1)}, f32[16,1024]{1,0:T(8,128)S(1)}, u32[]{:S(2)}, u32[]{:S(2)}) collective-permute-start(f32[16,1024]{1,0:T(8,128)S(1)} %get-tuple-element.323), channel_id=1, source_target_pairs={{0,1},{1,2},{2,3},{3,4},{4,5},{5,6},{6,7},{7,8},{8,9},{9,10},{10,1... | collective-permute-start | bytes 196616 | tf_op jit(solution)/shard_map/while/body/eval_jaxpr/ppermute | solution.py:15
  271.9 0.7 copy-start.1
where the time goes:
time: 274 us; the launch traced here: 273 us
  blocking collectives  210 us (77%)
  starting transfers between devices  33.5 us (12%)
  waiting for transfers between devices  22.5 us (8%)
  matrix products  3.59 us (1%)
    psum x3, blocking collectives, squares(): return lax.psum(local_inner(vector, vector), ('gx', 'gy', 'gz'))  126 us
    psum x2, blocking collectives, advance(): curvature = lax.psum(local_inner(direction, applied), ('gx', 'gy', 'gz'))  84.4 us
    ppermute x15, starting transfers between devices, passed_along(): lax.ppermute(value, axis, [(source, source + steps) for source in range(l...  33.5 us
    ppermute x15, waiting for transfers between devices, passed_along(): lax.ppermute(value, axis, [(source, source + steps) for source in range(l...  22.5 us
  transfers between devices with their start and end apart: 15, of which 12 were waited for; matrix products, arithmetic and copies ran while one was open for 0% of the time, Pallas kernels for 0%

commit v1 on v0

v1 whole, which is shorter than its diff:
```python
import functools

import jax
import jax.numpy as jnp
from jax import lax
from jax.experimental import pallas as pl
from jax.experimental.pallas import tpu as pltpu
from jax.sharding import PartitionSpec as P

MESH = pl.DeviceIdType.MESH
AXES = ("gx", "gy", "gz")
WELL_RATE = 4.0
SEND_ORDER = (1, 4, 2, 5, 0, 3)
TAKE_ORDER = (0, 3, 2, 5, 1, 4)


def kernel(extents, basis_hbm, diag_ref, source_ref, wells_ref, out_ref,
           basis, flux, resp, got, sums, plane, column,
           load_sem, send_sem, recv_sem, plane_send, plane_recv, col_send, col_recv):
    width = basis.shape[1] // 6
    cases = source_ref.shape[0]
    at = tuple(lax.axis_index(a) for a in AXES)
    nx, ny, nz = extents

    def cut(face):
        return slice(face * width, (face + 1) * width)

    loads = {}
    for face in SEND_ORDER:
        loads[face] = pltpu.make_async_copy(
            basis_hbm.at[:, cut(face)], basis.at[:, cut(face)], load_sem.at[face])
        loads[face].start()

    plane_peers = []
    for k in range(1, nx * ny):
        kx, ky = k // ny, k % ny
        plane_peers.append((lax.rem(at[0] + kx, nx), lax.rem(at[1] + ky, ny), at[2]))
    col_peers = [(at[0], at[1], lax.rem(at[2] + k, nz)) for k in range(1, nz)]

    barrier = pltpu.get_barrier_semaphore()
    for peer in plane_peers + col_peers:
        pl.semaphore_signal(barrier, inc=1, device_id=peer, device_id_type=MESH)

    eye = (lax.broadcasted_iota(jnp.int32, (cases, cases), 0)
           == lax.broadcasted_iota(jnp.int32, (cases, cases), 1))
    cells = jnp.sum(jnp.where(eye, wells_ref[...].astype(jnp.float32), 0.0), axis=1, keepdims=True)
    modes = lax.broadcasted_iota(jnp.int32, source_ref.shape, 1).astype(jnp.float32)
    load_low = (source_ref[...] + jnp.where(modes == cells, WELL_RATE, 0.0)).astype(jnp.bfloat16)

    def has(face):
        axis = face % 3
        return at[axis] < extents[axis] - 1 if face >= 3 else at[axis] > 0

    def message(phase, face, source):
        axis, upper = face % 3, face >= 3
        target = list(at)
        target[axis] = at[axis] + (1 if upper else -1)
        landing = axis if upper else 3 + axis
        return pltpu.make_async_remote_copy(
            src_ref=source.at[:, cut(face)],
            dst_ref=got.at[phase, :, cut(landing)],
            send_sem=send_sem.at[phase, face],
            recv_sem=recv_sem.at[phase, landing],
            device_id=tuple(target), device_id_type=MESH)

    def arrival(phase, face):
        return pltpu.make_async_remote_copy(
            src_ref=flux.at[:, cut(face)],
            dst_ref=got.at[phase, :, cut(face)],
            send_sem=send_sem.at[phase, face],
            recv_sem=recv_sem.at[phase, face],
            device_id=tuple(at), device_id_type=MESH)

    def send(phase, face, source):
        @pl.when(has(face))
        def _():
            message(phase, face, source).start()

    def finish(phase, face, source):
        @pl.when(has(face))
        def _():
            message(phase, face, source).wait_send()

    for i, face in enumerate(SEND_ORDER):
        loads[face].wait()
        flux[:, cut(face)] = jnp.dot(load_low, basis[:, cut(face)], preferred_element_type=jnp.float32)
        if i == 0:
            pl.semaphore_wait(barrier, len(plane_peers) + len(col_peers))
        send(0, face, flux)

    def to_modes(field, face):
        return lax.dot_general(field.astype(jnp.bfloat16), basis[:, cut(face)],
                               (((1,), (1,)), ((), ())), preferred_element_type=jnp.float32)

    def taken(phase, face, source):
        arrived = has(face)

        @pl.when(arrived)
        def _():
            arrival(phase, face).wait_recv()

        return jnp.where(arrived, source[:, cut(face)] + got[phase, :, cut(face)], 0.0)

    def fold(x):
        return functools.reduce(jnp.add, [x[:, i:i + 128] for i in range(0, width, 128)])

    field = {}
    mode_values = jnp.zeros((cases, basis.shape[0]), jnp.float32)
    rr = jnp.zeros((cases, 128), jnp.float32)
    rw = jnp.zeros((cases, 128), jnp.float32)
    for face in TAKE_ORDER:
        f = taken(0, face, flux)
        field[face] = f
        mode_values = mode_values + to_modes(f, face)
        squares = f * f
        if face < 3:
            rr = rr + fold(squares)
        rw = rw + fold(diag_ref[:, cut(face)] * squares)
    m_low = mode_values.astype(jnp.bfloat16)

    for face in SEND_ORDER:
        resp[:, cut(face)] = diag_ref[:, cut(face)] * field[face] + jnp.dot(
            m_low, basis[:, cut(face)], preferred_element_type=jnp.float32)
        send(1, face, resp)

    def total(x):
        return jnp.sum(x, axis=1, keepdims=True)

    rr = total(rr)
    m_wide = m_low.astype(jnp.float32)
    rw = total(rw) + total(m_wide * mode_values)

    mode_values = jnp.zeros((cases, basis.shape[0]), jnp.float32)
    ww = jnp.zeros((cases, 128), jnp.float32)
    dw = jnp.zeros((cases, 128), jnp.float32)
    image = {}
    for face in TAKE_ORDER:
        f = taken(1, face, resp)
        if face < 3:
            image[face] = f
        mode_values = mode_values + to_modes(f, face)
        squares = f * f
        if face < 3:
            ww = ww + fold(squares)
        dw = dw + fold(diag_ref[:, cut(face)] * squares)
    ww = total(ww)
    m_wide = mode_values.astype(jnp.bfloat16).astype(jnp.float32)
    waw = total(dw) + total(m_wide * mode_values)

    half = cases // 2
    lane = lax.broadcasted_iota(jnp.int32, (half, 128), 1)
    packed = jnp.zeros((half, 128), jnp.float32)
    for k, value in enumerate((rr, rw, ww, waw)):
        packed = jnp.where(lane == 2 * k, value[:half], packed)
        packed = jnp.where(lane == 2 * k + 1, value[half:], packed)

    def everyone(step, value, peers, slots, s_sem, r_sem):
        sums[step] = value
        copies = []
        for k, peer in enumerate(peers):
            copies.append(pltpu.make_async_remote_copy(
                src_ref=sums.at[step], dst_ref=slots.at[k],
                send_sem=s_sem.at[k], recv_sem=r_sem.at[k],
                device_id=peer, device_id_type=MESH))
            copies[-1].start()
        for k, copy in enumerate(copies):
            copy.wait_recv()
            value = value + slots[k]
        return value, copies

    packed, copies0 = everyone(0, packed, plane_peers, plane, plane_send, plane_recv)
    packed, copies1 = everyone(1, packed, col_peers, column, col_send, col_recv)

    def value_of(k):
        return jnp.concatenate([packed[:, 2 * k:2 * k + 1], packed[:, 2 * k + 1:2 * k + 2]], axis=0)

    rr, rw, ww, waw = (value_of(k) for k in range(4))
    a0 = rr / rw
    norm1 = rr - 2.0 * a0 * rw + a0 * a0 * ww
    grow = 1.0 + norm1 / rr
    a1 = norm1 / (grow * grow * rw - 2.0 * grow * a0 * ww + a0 * a0 * waw)
    c_b = a0 + a1 * grow
    c_w = a0 * a1
    for face in range(3):
        out_ref[:, cut(face)] = c_b * field[face] - c_w * image[face]

    for face in SEND_ORDER:
        finish(0, face, flux)
        finish(1, face, resp)
    for copy in copies0 + copies1:
        copy.wait_send()


def solution(mesh):
    extents = tuple(mesh.shape[a] for a in AXES)

    def body(basis, diagonal, source, well_cells):
        modes, columns = basis.shape[-2:]
        cases = source.shape[-2]
        vmem = pl.BlockSpec(memory_space=pltpu.VMEM)
        dma = pltpu.SemaphoreType.DMA
        plane_count, col_count = extents[0] * extents[1] - 1, extents[2] - 1
        out = pl.pallas_call(
            functools.partial(kernel, extents),
            out_shape=jax.ShapeDtypeStruct((cases, columns // 2), jnp.float32),
            in_specs=[pl.BlockSpec(memory_space=pl.ANY), vmem, vmem, vmem],
            out_specs=vmem,
            scratch_shapes=[
                pltpu.VMEM((modes, columns), jnp.bfloat16),
                pltpu.VMEM((cases, columns), jnp.float32),
                pltpu.VMEM((cases, columns), jnp.float32),
                pltpu.VMEM((2, cases, columns), jnp.float32),
                pltpu.VMEM((2, cases // 2, 128), jnp.float32),
                pltpu.VMEM((plane_count, cases // 2, 128), jnp.float32),
                pltpu.VMEM((col_count, cases // 2, 128), jnp.float32),
                dma((6,)), dma((2, 6)), dma((2, 6)),
                dma((plane_count,)), dma((plane_count,)),
                dma((col_count,)), dma((col_count,)),
            ],
            compiler_params=pltpu.CompilerParams(
                collective_id=0, has_side_effects=True, vmem_limit_bytes=32 * 2**20),
        )(
            basis.reshape(modes, columns),
            diagonal.reshape(1, columns),
            source.reshape(cases, modes),
            well_cells.reshape(1, cases),
        )
        return out.reshape((1, 1, 1) + out.shape)

    in_specs = (
        P("gx", "gy", "gz", None, None),
        P("gx", "gy", "gz", None),
        P("gx", "gy", "gz", None, None),
        P("gx", "gy", "gz", None),
    )
    out_specs = P("gx", "gy", "gz", None, None)
    return jax.shard_map(body, mesh=mesh, in_specs=in_specs, out_specs=out_specs, check_vma=False)
```

time: 274 us -> 27.4 us (0.10)
  blocking collectives: 210 us -> 0 us
  starting transfers between devices: 33.5 us -> 0 us
  Pallas kernels: 0 us -> 23.1 us
  waiting for transfers between devices: 22.5 us -> 0 us
  matrix products: 3.59 us -> 0 us
  local copies, waits for them, and re-layouts: 0.74 us -> 4.04 us
    psum x5 -> x0, blocking collectives: 210 us -> none  [the longest x3 126 us: squares(): return lax.psum(local_inner(vector, vector), ('gx', 'gy', 'gz'))]
    ppermute x15 -> x0, starting transfers between devices: 33.5 us -> none  [passed_along(): lax.ppermute(value, axis, [(source, source + steps) for source in range(l...]
    pallas_call x0 -> x1, Pallas kernels: none -> 23.1 us  [body(): pl.pallas_call(functools.partial(kernel, extents), out_shape=jax.ShapeDty...]
    ppermute x15 -> x0, waiting for transfers between devices: 22.5 us -> none  [passed_along(): lax.ppermute(value, axis, [(source, source + steps) for source in range(l...]
    dot_general x3 -> x0, matrix products: 3.59 us -> none  [the longest x2 1.96 us: respond(): jnp.dot(mode_values, basis_local, preferred_element_type=jnp.float32)]
    unnamed x7 -> x9, local copies, waits for them, and re-layouts: 0.69 us -> 4.04 us
  transfers between devices with their start and end apart: 15 -> 0, of which waited for: 12 -> 0; matrix products, arithmetic and copies ran while one was open for 0% -> 0% of each run, Pallas kernels for 0% -> 0%
where the time goes in v1:
time: 27.4 us; the launch traced here: 27.1 us
  Pallas kernels  23.1 us (84%)
  local copies, waits for them, and re-layouts  4.04 us (15%)
    pallas_call x1, Pallas kernels, body(): pl.pallas_call(functools.partial(kernel, extents), out_shape=jax.ShapeDty...  23.1 us
    unnamed x9, local copies, waits for them, and re-layouts  4.04 us

profile of v1, /device:TPU:0, one launch (start us, length us, event | category | flops | bytes accessed | tf_op | source)
XLA Modules:
  0.0 27.1 jit_solution(15242862549097634936)
XLA Ops:
  0.0 0.0 copy-start
  0.0 1.3 %copy-done = bf16[1,1,1,96,6144]{4,3,2,1,0:T(8,128)(2,1)S(1)} copy-done((bf16[1,1,1,96,6144]{4,3,2,1,0:T(8,128)(2,1)S(1)}, bf16[1,1,1,96,6144]{4,3,2,1,0:T(8,128)(2,1)}, u32[]{:S(2)}) %copy-start) | copy-done | bytes 1179672
  1.3 0.0 copy-start.1
  1.3 0.7 %copy-done.1 = f32[1,1,1,6144]{3,2,1,0:T(1,128)S(1)} copy-done((f32[1,1,1,6144]{3,2,1,0:T(1,128)S(1)}, f32[1,1,1,6144]{3,2,1,0:T(1,128)}, u32[]{:S(2)}) %copy-start.1) | copy-done | bytes 24600
  2.0 0.0 copy-start.2
  2.0 0.7 %copy-done.2 = f32[1,1,1,16,96]{4,3,2,1,0:T(8,128)S(1)} copy-done((f32[1,1,1,16,96]{4,3,2,1,0:T(8,128)S(1)}, f32[1,1,1,16,96]{4,3,2,1,0:T(8,128)}, u32[]{:S(2)}) %copy-start.2) | copy-done | bytes 6168
  2.7 0.0 copy-start.3
  2.7 0.7 %copy-done.3 = s32[1,1,1,16]{3,2,1,0:T(1,128)S(1)} copy-done((s32[1,1,1,16]{3,2,1,0:T(1,128)S(1)}, s32[1,1,1,16]{3,2,1,0:T(1,128)}, u32[]{:S(2)}) %copy-start.3) | copy-done | bytes 88
  3.4 23.1 %shard_map.46 = f32[16,3072]{1,0:T(8,128)S(1)} custom-call(bf16[96,6144]{1,0:T(8,128)(2,1)S(1)} %bitcast.5, f32[1,6144]{1,0:T(1,128)S(1)} %bitcast.7, f32[16,96]{1,0:T(8,128)S(1)} %bitcast.8, s32[1,16]{1,0:T(1,128)S(1)} %bitcast.9), custom_call_target="tpu_custom_call" | custom-call | tf_op jit(solution)/shard_map/pallas_call | solution.py:203
  26.5 0.7 %copy.6 = f32[1,1,1,16,3072]{4,3,2,1,0:T(8,128)} copy(f32[1,1,1,16,3072]{4,3,2,1,0:T(8,128)S(1)} %bitcast.6) | data formatting | bytes 393216
Async XLA Ops:
  0.0 1.3 %copy-start = (bf16[1,1,1,96,6144]{4,3,2,1,0:T(8,128)(2,1)S(1)}, bf16[1,1,1,96,6144]{4,3,2,1,0:T(8,128)(2,1)}, u32[]{:S(2)}) copy-start(bf16[1,1,1,96,6144]{4,3,2,1,0:T(8,128)(2,1)} %param.4) | copy-start | bytes 3538948
  1.3 0.7 %copy-start.1 = (f32[1,1,1,6144]{3,2,1,0:T(1,128)S(1)}, f32[1,1,1,6144]{3,2,1,0:T(1,128)}, u32[]{:S(2)}) copy-start(f32[1,1,1,6144]{3,2,1,0:T(1,128)} %param.5) | copy-start | bytes 73732
  2.0 0.7 %copy-start.2 = (f32[1,1,1,16,96]{4,3,2,1,0:T(8,128)S(1)}, f32[1,1,1,16,96]{4,3,2,1,0:T(8,128)}, u32[]{:S(2)}) copy-start(f32[1,1,1,16,96]{4,3,2,1,0:T(8,128)} %param.6) | copy-start | bytes 18436
  2.7 0.7 %copy-start.3 = (s32[1,1,1,16]{3,2,1,0:T(1,128)S(1)}, s32[1,1,1,16]{3,2,1,0:T(1,128)}, u32[]{:S(2)}) copy-start(s32[1,1,1,16]{3,2,1,0:T(1,128)} %param.7) | copy-start | bytes 196

commit v2 on v1

--- a/solution.py
+++ b/solution.py
@@ -14,9 +14,9 @@
 TAKE_ORDER = (0, 3, 2, 5, 1, 4)
 
 
-def kernel(extents, basis_hbm, diag_ref, source_ref, wells_ref, out_ref,
-           basis, flux, resp, got, sums, plane, column,
-           load_sem, send_sem, recv_sem, plane_send, plane_recv, col_send, col_recv):
+def kernel(extents, basis_hbm, diag_hbm, source_hbm, wells_hbm, out_ref,
+           basis, diag_ref, source_ref, wells_ref, flux, resp, got, mine, theirs,
+           load_sem, small_sem, send_sem, recv_sem, sum_send, sum_recv):
     width = basis.shape[1] // 6
     cases = source_ref.shape[0]
     at = tuple(lax.axis_index(a) for a in AXES)
@@ -25,22 +25,28 @@
     def cut(face):
         return slice(face * width, (face + 1) * width)
 
+    small = [pltpu.make_async_copy(a, b, small_sem.at[i]) for i, (a, b) in enumerate((
+        (source_hbm, source_ref), (wells_hbm, wells_ref), (diag_hbm, diag_ref)))]
+    small[0].start()
+    small[1].start()
     loads = {}
     for face in SEND_ORDER:
         loads[face] = pltpu.make_async_copy(
             basis_hbm.at[:, cut(face)], basis.at[:, cut(face)], load_sem.at[face])
         loads[face].start()
-
-    plane_peers = []
-    for k in range(1, nx * ny):
-        kx, ky = k // ny, k % ny
-        plane_peers.append((lax.rem(at[0] + kx, nx), lax.rem(at[1] + ky, ny), at[2]))
-    col_peers = [(at[0], at[1], lax.rem(at[2] + k, nz)) for k in range(1, nz)]
+    small[2].start()
+
+    peers = []
+    for k in reversed(range(1, nx * ny * nz)):
+        kz, ky, kx = k // (nx * ny), k // nx % ny, k % nx
+        peers.append((lax.rem(at[0] + kx, nx), lax.rem(at[1] + ky, ny), lax.rem(at[2] + kz, nz)))
 
     barrier = pltpu.get_barrier_semaphore()
-    for peer in plane_peers + col_peers:
+    for peer in peers:
         pl.semaphore_signal(barrier, inc=1, device_id=peer, device_id_type=MESH)
 
+    small[0].wait()
+    small[1].wait()
     eye = (lax.broadcasted_iota(jnp.int32, (cases, cases), 0)
            == lax.broadcasted_iota(jnp.int32, (cases, cases), 1))
     cells = jnp.sum(jnp.where(eye, wells_ref[...].astype(jnp.float32), 0.0), axis=1, keepdims=True)
@@ -85,7 +91,7 @@
         loads[face].wait()
         flux[:, cut(face)] = jnp.dot(load_low, basis[:, cut(face)], preferred_element_type=jnp.float32)
         if i == 0:
-            pl.semaphore_wait(barrier, len(plane_peers) + len(col_peers))
+            pl.semaphore_wait(barrier, len(peers))
         send(0, face, flux)
 
     def to_modes(field, face):
@@ -104,6 +110,7 @@
     def fold(x):
         return functools.reduce(jnp.add, [x[:, i:i + 128] for i in range(0, width, 128)])
 
+    small[2].wait()
     field = {}
     mode_values = jnp.zeros((cases, basis.shape[0]), jnp.float32)
     rr = jnp.zeros((cases, 128), jnp.float32)
@@ -147,32 +154,25 @@
     m_wide = mode_values.astype(jnp.bfloat16).astype(jnp.float32)
     waw = total(dw) + total(m_wide * mode_values)
 
-    half = cases // 2
-    lane = lax.broadcasted_iota(jnp.int32, (half, 128), 1)
-    packed = jnp.zeros((half, 128), jnp.float32)
+    lane = lax.broadcasted_iota(jnp.int32, (cases, 128), 1)
+    row = lax.broadcasted_iota(jnp.int32, (cases, 128), 0)
+    spread = jnp.zeros((cases, 128), jnp.float32)
     for k, value in enumerate((rr, rw, ww, waw)):
-        packed = jnp.where(lane == 2 * k, value[:half], packed)
-        packed = jnp.where(lane == 2 * k + 1, value[half:], packed)
-
-    def everyone(step, value, peers, slots, s_sem, r_sem):
-        sums[step] = value
-        copies = []
-        for k, peer in enumerate(peers):
-            copies.append(pltpu.make_async_remote_copy(
-                src_ref=sums.at[step], dst_ref=slots.at[k],
-                send_sem=s_sem.at[k], recv_sem=r_sem.at[k],
-                device_id=peer, device_id_type=MESH))
-            copies[-1].start()
-        for k, copy in enumerate(copies):
-            copy.wait_recv()
-            value = value + slots[k]
-        return value, copies
-
-    packed, copies0 = everyone(0, packed, plane_peers, plane, plane_send, plane_recv)
-    packed, copies1 = everyone(1, packed, col_peers, column, col_send, col_recv)
+        spread = jnp.where(lane == row + k * cases, value, spread)
+    mine[...] = jnp.sum(spread, axis=0, keepdims=True)
+    copies = []
+    for k, peer in enumerate(peers):
+        copies.append(pltpu.make_async_remote_copy(
+            src_ref=mine, dst_ref=theirs.at[k],
+            send_sem=sum_send.at[k], recv_sem=sum_recv.at[k],
+            device_id=peer, device_id_type=MESH))
+        copies[-1].start()
+    for copy in copies:
+        copy.wait_recv()
+    summed = mine[...] + jnp.sum(theirs[...], axis=0)
 
     def value_of(k):
-        return jnp.concatenate([packed[:, 2 * k:2 * k + 1], packed[:, 2 * k + 1:2 * k + 2]], axis=0)
+        return total(jnp.where(lane == row + k * cases, summed, 0.0))
 
     rr, rw, ww, waw = (value_of(k) for k in range(4))
     a0 = rr / rw
@@ -187,7 +187,7 @@
     for face in SEND_ORDER:
         finish(0, face, flux)
         finish(1, face, resp)
-    for copy in copies0 + copies1:
+    for copy in copies:
         copy.wait_send()
 
 
@@ -199,26 +199,27 @@
         cases = source.shape[-2]
         vmem = pl.BlockSpec(memory_space=pltpu.VMEM)
         dma = pltpu.SemaphoreType.DMA
-        plane_count, col_count = extents[0] * extents[1] - 1, extents[2] - 1
+        others = extents[0] * extents[1] * extents[2] - 1
         out = pl.pallas_call(
             functools.partial(kernel, extents),
-            out_shape=jax.ShapeDtypeStruct((cases, columns // 2), jnp.float32),
-            in_specs=[pl.BlockSpec(memory_space=pl.ANY), vmem, vmem, vmem],
+            out_shape=pltpu.VMEM((cases, columns // 2), jnp.float32),
+            in_specs=[pl.BlockSpec(memory_space=pl.ANY)] * 4,
             out_specs=vmem,
             scratch_shapes=[
                 pltpu.VMEM((modes, columns), jnp.bfloat16),
+                pltpu.VMEM((1, columns), jnp.float32),
+                pltpu.VMEM((cases, modes), jnp.float32),
+                pltpu.VMEM((1, cases), jnp.int32),
                 pltpu.VMEM((cases, columns), jnp.float32),
                 pltpu.VMEM((cases, columns), jnp.float32),
                 pltpu.VMEM((2, cases, columns), jnp.float32),
-                pltpu.VMEM((2, cases // 2, 128), jnp.float32),
-                pltpu.VMEM((plane_count, cases // 2, 128), jnp.float32),
-                pltpu.VMEM((col_count, cases // 2, 128), jnp.float32),
-                dma((6,)), dma((2, 6)), dma((2, 6)),
-                dma((plane_count,)), dma((plane_count,)),
-                dma((col_count,)), dma((col_count,)),
+                pltpu.VMEM((1, 128), jnp.float32),
+                pltpu.VMEM((others, 1, 128), jnp.float32),
+                dma((6,)), dma((3,)), dma((2, 6)), dma((2, 6)),
+                dma((others,)), dma((others,)),
             ],
             compiler_params=pltpu.CompilerParams(
-                collective_id=0, has_side_effects=True, vmem_limit_bytes=32 * 2**20),
+                collective_id=0, has_side_effects=True, vmem_limit_bytes=60 * 2**20),
         )(
             basis.reshape(modes, columns),
             diagonal.reshape(1, columns),

time: 27.4 us -> 22 us (0.80)
  local copies, waits for them, and re-layouts: 4.04 us -> 0.68 us
  Pallas kernels: 23.1 us -> 21.2 us
    unnamed x9 -> x1, local copies, waits for them, and re-layouts: 4.04 us -> 0.68 us
    pallas_call x1, Pallas kernels: 23.1 us -> 21.2 us  [body(): pl.pallas_call(functools.partial(kernel, extents), out_shape=pltpu.VMEM((...]
where the time goes in v2:
time: 22 us; the launch traced here: 21.9 us
  Pallas kernels  21.2 us (96%)
  local copies, waits for them, and re-layouts  0.68 us (3%)
    pallas_call x1, Pallas kernels, body(): pl.pallas_call(functools.partial(kernel, extents), out_shape=pltpu.VMEM((...  21.2 us
    unnamed x1, local copies, waits for them, and re-layouts  0.68 us

profile of v2, /device:TPU:0, one launch (start us, length us, event | category | flops | bytes accessed | tf_op | source)
XLA Modules:
  0.0 21.9 jit_solution(12214363713816758593)
XLA Ops:
  0.0 21.2 %shard_map.46 = f32[16,3072]{1,0:T(8,128)S(1)} custom-call(bf16[96,6144]{1,0:T(8,128)(2,1)} %bitcast.6, f32[1,6144]{1,0:T(1,128)} %bitcast.7, f32[16,96]{1,0:T(8,128)} %bitcast.8, s32[1,16]{1,0:T(1,128)} %bitcast.9), custom_call_target="tpu_custom_call" | custom-call | tf_op jit(solution)/shard_map/pallas_call | solution.py:203
  21.2 0.7 %copy.6 = f32[1,1,1,16,3072]{4,3,2,1,0:T(8,128)} copy(f32[1,1,1,16,3072]{4,3,2,1,0:T(8,128)S(1)} %bitcast.5) | data formatting | bytes 393216

commit v3 on v2

--- a/solution.py
+++ b/solution.py
@@ -16,7 +16,7 @@
 
 def kernel(extents, basis_hbm, diag_hbm, source_hbm, wells_hbm, out_ref,
            basis, diag_ref, source_ref, wells_ref, flux, resp, got, mine, theirs,
-           load_sem, small_sem, send_sem, recv_sem, sum_send, sum_recv):
+           load_sem, small_sem, send_sem, recv_sem, sum_send, sum_recv, y_known, z_known):
     width = basis.shape[1] // 6
     cases = source_ref.shape[0]
     at = tuple(lax.axis_index(a) for a in AXES)
@@ -41,8 +41,17 @@
         kz, ky, kx = k // (nx * ny), k // nx % ny, k % nx
         peers.append((lax.rem(at[0] + kx, nx), lax.rem(at[1] + ky, ny), lax.rem(at[2] + kz, nz)))
 
+    x_peers = [(lax.rem(at[0] + k, nx), at[1], at[2]) for k in range(1, nx)]
+    y_peers = [(at[0], lax.rem(at[1] + k, ny), at[2]) for k in range(1, ny)]
+    z_peers = [(at[0], at[1], lax.rem(at[2] + k, nz)) for k in range(1, nz)]
+    greeted = y_peers + z_peers + x_peers
+
+    def tell(known, some):
+        for peer in some:
+            pl.semaphore_signal(known, inc=1, device_id=peer, device_id_type=MESH)
+
     barrier = pltpu.get_barrier_semaphore()
-    for peer in peers:
+    for peer in greeted:
         pl.semaphore_signal(barrier, inc=1, device_id=peer, device_id_type=MESH)
 
     small[0].wait()
@@ -82,6 +91,19 @@
         def _():
             message(phase, face, source).start()
 
+    def send_pair(phase, source):
+        odd = lax.rem(at[1], 2) == 1
+
+        @pl.when(odd)
+        def _():
+            send(phase, 4, source)
+            send(phase, 1, source)
+
+        @pl.when(jnp.logical_not(odd))
+        def _():
+            send(phase, 1, source)
+            send(phase, 4, source)
+
     def finish(phase, face, source):
         @pl.when(has(face))
         def _():
@@ -91,8 +113,13 @@
         loads[face].wait()
         flux[:, cut(face)] = jnp.dot(load_low, basis[:, cut(face)], preferred_element_type=jnp.float32)
         if i == 0:
-            pl.semaphore_wait(barrier, len(peers))
-        send(0, face, flux)
+            pl.semaphore_wait(barrier, len(greeted))
+        if face == 4:
+            send_pair(0, flux)
+        elif face != 1:
+            send(0, face, flux)
+
+    tell(y_known, y_peers)
 
     def to_modes(field, face):
         return lax.dot_general(field.astype(jnp.bfloat16), basis[:, cut(face)],
@@ -128,7 +155,13 @@
     for face in SEND_ORDER:
         resp[:, cut(face)] = diag_ref[:, cut(face)] * field[face] + jnp.dot(
             m_low, basis[:, cut(face)], preferred_element_type=jnp.float32)
-        send(1, face, resp)
+        if face == 4:
+            send_pair(1, resp)
+        elif face != 1:
+            send(1, face, resp)
+
+    pl.semaphore_wait(y_known, len(y_peers))
+    tell(z_known, z_peers)
 
     def total(x):
         return jnp.sum(x, axis=1, keepdims=True)
@@ -160,6 +193,7 @@
     for k, value in enumerate((rr, rw, ww, waw)):
         spread = jnp.where(lane == row + k * cases, value, spread)
     mine[...] = jnp.sum(spread, axis=0, keepdims=True)
+    pl.semaphore_wait(z_known, len(z_peers))
     copies = []
     for k, peer in enumerate(peers):
         copies.append(pltpu.make_async_remote_copy(
@@ -217,6 +251,7 @@
                 pltpu.VMEM((others, 1, 128), jnp.float32),
                 dma((6,)), dma((3,)), dma((2, 6)), dma((2, 6)),
                 dma((others,)), dma((others,)),
+                pltpu.SemaphoreType.REGULAR, pltpu.SemaphoreType.REGULAR,
             ],
             compiler_params=pltpu.CompilerParams(
                 collective_id=0, has_side_effects=True, vmem_limit_bytes=60 * 2**20),

time: 22 us -> 20.7 us (0.941)
  Pallas kernels: 21.2 us -> 19.8 us
    pallas_call x1, Pallas kernels: 21.2 us -> 19.8 us  [body(): pl.pallas_call(functools.partial(kernel, extents), out_shape=pltpu.VMEM((...]
where the time goes in v3:
time: 20.7 us; the launch traced here: 20.5 us
  Pallas kernels  19.8 us (96%)
  local copies, waits for them, and re-layouts  0.68 us (3%)
    pallas_call x1, Pallas kernels, body(): pl.pallas_call(functools.partial(kernel, extents), out_shape=pltpu.VMEM((...  19.8 us
    unnamed x1, local copies, waits for them, and re-layouts  0.68 us

profile of v3, /device:TPU:0, one launch (start us, length us, event | category | flops | bytes accessed | tf_op | source)
XLA Modules:
  0.0 20.5 jit_solution(12512510245302701197)
XLA Ops:
  0.0 19.8 %shard_map.46 = f32[16,3072]{1,0:T(8,128)S(1)} custom-call(bf16[96,6144]{1,0:T(8,128)(2,1)} %bitcast.6, f32[1,6144]{1,0:T(1,128)} %bitcast.7, f32[16,96]{1,0:T(8,128)} %bitcast.8, s32[1,16]{1,0:T(1,128)} %bitcast.9), custom_call_target="tpu_custom_call" | custom-call | tf_op jit(solution)/shard_map/pallas_call | solution.py:237
  19.8 0.7 %copy.6 = f32[1,1,1,16,3072]{4,3,2,1,0:T(8,128)} copy(f32[1,1,1,16,3072]{4,3,2,1,0:T(8,128)S(1)} %bitcast.5) | data formatting | bytes 393216

commit v4 on v3

--- a/solution.py
+++ b/solution.py
@@ -194,15 +194,16 @@
         spread = jnp.where(lane == row + k * cases, value, spread)
     mine[...] = jnp.sum(spread, axis=0, keepdims=True)
     pl.semaphore_wait(z_known, len(z_peers))
-    copies = []
     for k, peer in enumerate(peers):
-        copies.append(pltpu.make_async_remote_copy(
+        pltpu.make_async_remote_copy(
             src_ref=mine, dst_ref=theirs.at[k],
-            send_sem=sum_send.at[k], recv_sem=sum_recv.at[k],
-            device_id=peer, device_id_type=MESH))
-        copies[-1].start()
-    for copy in copies:
-        copy.wait_recv()
+            send_sem=sum_send, recv_sem=sum_recv,
+            device_id=peer, device_id_type=MESH).start()
+    for face in SEND_ORDER:
+        finish(0, face, flux)
+        finish(1, face, resp)
+    pltpu.make_async_copy(theirs, theirs, sum_send).wait()
+    pltpu.make_async_copy(theirs, theirs, sum_recv).wait()
     summed = mine[...] + jnp.sum(theirs[...], axis=0)
 
     def value_of(k):
@@ -217,12 +218,6 @@
     c_w = a0 * a1
     for face in range(3):
         out_ref[:, cut(face)] = c_b * field[face] - c_w * image[face]
-
-    for face in SEND_ORDER:
-        finish(0, face, flux)
-        finish(1, face, resp)
-    for copy in copies:
-        copy.wait_send()
 
 
 def solution(mesh):
@@ -250,7 +245,7 @@
                 pltpu.VMEM((1, 128), jnp.float32),
                 pltpu.VMEM((others, 1, 128), jnp.float32),
                 dma((6,)), dma((3,)), dma((2, 6)), dma((2, 6)),
-                dma((others,)), dma((others,)),
+                dma, dma,
                 pltpu.SemaphoreType.REGULAR, pltpu.SemaphoreType.REGULAR,
             ],
             compiler_params=pltpu.CompilerParams(

time: 20.7 us -> 20 us (0.966)
  Pallas kernels: 19.8 us -> 19.2 us
    pallas_call x1, Pallas kernels: 19.8 us -> 19.2 us  [body(): pl.pallas_call(functools.partial(kernel, extents), out_shape=pltpu.VMEM((...]
where the time goes in v4:
time: 20 us; the launch traced here: 19.9 us
  Pallas kernels  19.2 us (96%)
  local copies, waits for them, and re-layouts  0.68 us (3%)
    pallas_call x1, Pallas kernels, body(): pl.pallas_call(functools.partial(kernel, extents), out_shape=pltpu.VMEM((...  19.2 us
    unnamed x1, local copies, waits for them, and re-layouts  0.68 us

profile of v4, /device:TPU:0, one launch (start us, length us, event | category | flops | bytes accessed | tf_op | source)
XLA Modules:
  0.0 19.9 jit_solution(17822133039997471432)
XLA Ops:
  0.0 19.2 %shard_map.46 = f32[16,3072]{1,0:T(8,128)S(1)} custom-call(bf16[96,6144]{1,0:T(8,128)(2,1)} %bitcast.6, f32[1,6144]{1,0:T(1,128)} %bitcast.7, f32[16,96]{1,0:T(8,128)} %bitcast.8, s32[1,16]{1,0:T(1,128)} %bitcast.9), custom_call_target="tpu_custom_call" | custom-call | tf_op jit(solution)/shard_map/pallas_call | solution.py:232
  19.2 0.7 %copy.6 = f32[1,1,1,16,3072]{4,3,2,1,0:T(8,128)} copy(f32[1,1,1,16,3072]{4,3,2,1,0:T(8,128)S(1)} %bitcast.5) | data formatting | bytes 393216

commit v5 on v4

--- a/solution.py
+++ b/solution.py
@@ -15,7 +15,7 @@
 
 
 def kernel(extents, basis_hbm, diag_hbm, source_hbm, wells_hbm, out_ref,
-           basis, diag_ref, source_ref, wells_ref, flux, resp, got, mine, theirs,
+           basis, turned, diag_ref, source_ref, wells_ref, flux, resp, got, mine, theirs,
            load_sem, small_sem, send_sem, recv_sem, sum_send, sum_recv, y_known, z_known):
     width = basis.shape[1] // 6
     cases = source_ref.shape[0]
@@ -24,6 +24,24 @@
 
     def cut(face):
         return slice(face * width, (face + 1) * width)
+
+    peers = []
+    for k in reversed(range(1, nx * ny * nz)):
+        kz, ky, kx = k // (nx * ny), k // nx % ny, k % nx
+        peers.append((lax.rem(at[0] + kx, nx), lax.rem(at[1] + ky, ny), lax.rem(at[2] + kz, nz)))
+
+    x_peers = [(lax.rem(at[0] + k, nx), at[1], at[2]) for k in range(1, nx)]
+    y_peers = [(at[0], lax.rem(at[1] + k, ny), at[2]) for k in range(1, ny)]
+    z_peers = [(at[0], at[1], lax.rem(at[2] + k, nz)) for k in range(1, nz)]
+    greeted = y_peers + z_peers + x_peers
+
+    def tell(known, some):
+        for peer in some:
+            pl.semaphore_signal(known, inc=1, device_id=peer, device_id_type=MESH)
+
+    barrier = pltpu.get_barrier_semaphore()
+    for peer in greeted:
+        pl.semaphore_signal(barrier, inc=1, device_id=peer, device_id_type=MESH)
 
     small = [pltpu.make_async_copy(a, b, small_sem.at[i]) for i, (a, b) in enumerate((
         (source_hbm, source_ref), (wells_hbm, wells_ref), (diag_hbm, diag_ref)))]
@@ -35,24 +53,6 @@
             basis_hbm.at[:, cut(face)], basis.at[:, cut(face)], load_sem.at[face])
         loads[face].start()
     small[2].start()
-
-    peers = []
-    for k in reversed(range(1, nx * ny * nz)):
-        kz, ky, kx = k // (nx * ny), k // nx % ny, k % nx
-        peers.append((lax.rem(at[0] + kx, nx), lax.rem(at[1] + ky, ny), lax.rem(at[2] + kz, nz)))
-
-    x_peers = [(lax.rem(at[0] + k, nx), at[1], at[2]) for k in range(1, nx)]
-    y_peers = [(at[0], lax.rem(at[1] + k, ny), at[2]) for k in range(1, ny)]
-    z_peers = [(at[0], at[1], lax.rem(at[2] + k, nz)) for k in range(1, nz)]
-    greeted = y_peers + z_peers + x_peers
-
-    def tell(known, some):
-        for peer in some:
-            pl.semaphore_signal(known, inc=1, device_id=peer, device_id_type=MESH)
-
-    barrier = pltpu.get_barrier_semaphore()
-    for peer in greeted:
-        pl.semaphore_signal(barrier, inc=1, device_id=peer, device_id_type=MESH)
 
     small[0].wait()
     small[1].wait()
@@ -111,6 +111,7 @@
 
     for i, face in enumerate(SEND_ORDER):
         loads[face].wait()
+        turned[cut(face), :] = basis[:, cut(face)].T
         flux[:, cut(face)] = jnp.dot(load_low, basis[:, cut(face)], preferred_element_type=jnp.float32)
         if i == 0:
             pl.semaphore_wait(barrier, len(greeted))
@@ -122,8 +123,8 @@
     tell(y_known, y_peers)
 
     def to_modes(field, face):
-        return lax.dot_general(field.astype(jnp.bfloat16), basis[:, cut(face)],
-                               (((1,), (1,)), ((), ())), preferred_element_type=jnp.float32)
+        return jnp.dot(field.astype(jnp.bfloat16), turned[cut(face), :],
+                       preferred_element_type=jnp.float32)
 
     def taken(phase, face, source):
         arrived = has(face)
@@ -236,6 +237,7 @@
             out_specs=vmem,
             scratch_shapes=[
                 pltpu.VMEM((modes, columns), jnp.bfloat16),
+                pltpu.VMEM((columns, modes), jnp.bfloat16),
                 pltpu.VMEM((1, columns), jnp.float32),
                 pltpu.VMEM((cases, modes), jnp.float32),
                 pltpu.VMEM((1, cases), jnp.int32),

time: 20 us -> 20.1 us (level)
  no operation moved by 1% of the time
where the time goes in v5:
time: 20.1 us; the launch traced here: 20 us
  Pallas kernels  19.3 us (96%)
  local copies, waits for them, and re-layouts  0.68 us (3%)
    pallas_call x1, Pallas kernels, body(): pl.pallas_call(functools.partial(kernel, extents), out_shape=pltpu.VMEM((...  19.3 us
    unnamed x1, local copies, waits for them, and re-layouts  0.68 us

profile of v5, /device:TPU:0, one launch (start us, length us, event | category | flops | bytes accessed | tf_op | source)
XLA Modules:
  0.0 20.0 jit_solution(5670707183931297019)
XLA Ops:
  0.0 19.3 %shard_map.46 = f32[16,3072]{1,0:T(8,128)S(1)} custom-call(bf16[96,6144]{1,0:T(8,128)(2,1)} %bitcast.6, f32[1,6144]{1,0:T(1,128)} %bitcast.7, f32[16,96]{1,0:T(8,128)} %bitcast.8, s32[1,16]{1,0:T(1,128)} %bitcast.9), custom_call_target="tpu_custom_call" | custom-call | tf_op jit(solution)/shard_map/pallas_call | solution.py:233
  19.3 0.7 %copy.6 = f32[1,1,1,16,3072]{4,3,2,1,0:T(8,128)} copy(f32[1,1,1,16,3072]{4,3,2,1,0:T(8,128)S(1)} %bitcast.5) | data formatting | bytes 393216
